TPU v7x, 128 devices: a whole 4x4x4 slice. The times are simulated.
128 devices in a mesh: energy: 8 (over x, core), length: 16 (over y, z).
Axes of the slice: x: 4, y: 4, z: 4, core: 2. Of those that a mesh axis runs over, the one named last changes fastest.
Arguments:
- green_left: float32 [8, 64, 2, 512, 512], P('energy', 'length')
- coupling: float32 [64, 512, 512], P('length')
- pattern: int32 [64, 8, 8], P('length'), may hold values from 0 to 1, as said below
- injection: float32 [8, 2, 512, 64], P('energy'), may hold values from -6 to 6
- weights: float32 [8], P('energy'), may hold values from 0.5 to 2
Outputs:
- charge: float32 [64, 512], P('length', 'energy')
Inputs may be any that keep to these rules, and one draw needn't show every extreme that they name: `pattern`: in every block the tiles on the diagonal are 1.
All inputs are finite; a program needn't handle non-finite values.
Results may differ from a plain program's by a relative error of at most 0.00016.
Values sent between devices are 32-bit elements; how exact they have to be, the bound alone decides.
A program may use at most 128 MiB of HBM per device.

v0:
```python
import jax
import jax.numpy as jnp
from jax import lax
from jax.sharding import PartitionSpec as P


def carried_in(part, axis, combine, identity):
    count = lax.axis_size(axis)
    place = lax.axis_index(axis)
    ahead = count - 1 - place
    gathered = lax.all_gather(part, axis)
    state = jnp.zeros_like(part) + jnp.asarray(identity, part.dtype)

    def one(hop, state):
        source = count - 1 - hop
        return combine(state, lax.dynamic_index_in_dim(gathered, source, 0, False))

    return lax.fori_loop(0, ahead, one, state)


def complex_product(left_op, right_op):
    highest = lax.Precision.HIGHEST

    def product(first_op, second_op):
        return jnp.einsum(
            "eij,ejk->eik",
            first_op,
            second_op,
            precision=highest,
            preferred_element_type=jnp.float32,
        )

    real_part = product(left_op[:, 0], right_op[:, 0]) - product(left_op[:, 1], right_op[:, 1])
    imag_part = product(left_op[:, 0], right_op[:, 1]) + product(left_op[:, 1], right_op[:, 0])
    return jnp.stack([real_part, imag_part], axis=1)


def shards(green_left, coupling, pattern, injection, weights):
    blocks = coupling.shape[0]
    orbitals = coupling.shape[1]
    tile_count = pattern.shape[1]
    tile_size = orbitals // tile_count
    tile_mask = pattern.astype(jnp.float32)[:, :, None, :, None]
    used_coupling = (
        coupling.reshape(blocks, tile_count, tile_size, tile_count, tile_size) * tile_mask
    ).reshape(blocks, orbitals, orbitals)
    propagators = jnp.einsum(
        "ebcij,bjk->ebcik",
        green_left,
        used_coupling,
        precision=lax.Precision.HIGHEST,
        preferred_element_type=jnp.float32,
    )
    composite = propagators[:, 0]
    for block in range(1, blocks):
        composite = complex_product(composite, propagators[:, block])
    unit_map = jnp.stack(
        [jnp.eye(orbitals, dtype=jnp.float32), jnp.zeros((orbitals, orbitals), jnp.float32)]
    )
    identity_map = jnp.broadcast_to(unit_map, composite.shape)

    def compose_maps(upper_map, lower_map):
        return complex_product(lower_map, upper_map)

    suffix = carried_in(composite, "length", compose_maps, identity_map)
    wavefunction = complex_product(suffix, injection)
    densities = [None] * blocks
    for block in reversed(range(blocks)):
        wavefunction = complex_product(propagators[:, block], wavefunction)
        densities[block] = jnp.sum(wavefunction * wavefunction, axis=(1, 3))
    stacked = jnp.stack(densities, axis=1)
    factor = 1.0 / (injection.shape[3] * green_left.shape[0] * lax.axis_size("energy"))
    local_charge = (
        jnp.einsum(
            "e,ebr->br",
            weights,
            stacked,
            precision=lax.Precision.HIGHEST,
            preferred_element_type=jnp.float32,
        )
        * factor
    )
    return lax.psum_scatter(local_charge, "energy", scatter_dimension=1, tiled=True)


def solution(mesh):
    placed = (
        P("energy", "length", None, None, None),
        P("length", None, None),
        P("length", None, None),
        P("energy", None, None, None),
        P("energy"),
    )
    return jax.shard_map(
        shards, mesh=mesh, in_specs=placed, out_specs=P("length", "energy"), check_vma=False
    )
```

profile of v0, /device:TPU:1, one launch (start us, length us, event | category | flops | bytes accessed | tf_op | source)
XLA Modules:
  0.0 473.7 jit_solution(582339690661539597)
XLA Ops:
  7.3 3.8 mul.64
  11.1 7.5 %mul.65 = f32[4,512,512]{2,1,0:T(8,128)} reshape(f32[4,8,64,8,64]{4,3,2,1,0:T(8,128)} %mul.64) | data formatting | bytes 8388608 | tf_op jit(solution)/shard_map/mul | solution.py:45
  18.6 29.5 %fusion.16 = f32[1,4,2,512,512]{3,4,2,1,0:T(8,128)S(1)} fusion(f32[1,4,2,512,512]{4,3,2,1,0:T(8,128)} %param.7, f32[4,512,512]{2,1,0:T(8,128)} %param.8, f32[4,512,512]{2,1,0:T(8,128)} %mul.65), kind=kOutput, calls=%fused_computation.22 | convolution fusion | flops 12885950464 | bytes 25165824 | tf_op jit(solution)/shard_map/ebcij,bjk->ebcik/dot_general | solution.py:47
  49.1 3.6 fusion.38
  52.6 3.6 fusion.37
  56.2 3.6 convolution_subtract_fusion.3
  59.7 2.3 fusion.43
  62.0 1.9 fusion.47
  63.9 3.6 convolution_add_fusion.3
  67.5 1.9 convolution_subtract_fusion.2
  69.4 1.9 fusion.46
  71.2 1.9 fusion.48
  73.3 1.9 convolution_add_fusion.2
  75.1 1.9 fusion.22
  77.0 1.9 fusion.21
  81.5 199.5 %all-gather.3.cloned.1.call-done = f32[16,2,512,512]{3,2,1,0:T(8,128)} async-done(((f32[1,2,512,512]{3,2,1,0:T(8,128)}), f32[16,2,512,512]{3,2,1,0:T(8,128)}) %all-gather.3.cloned.1.call-update) | async-done | bytes 33554448 | tf_op jit(solution)/shard_map/all_gather | solution.py:11
  281.0 141.7 %while.12 = (s32[]{:T(128)}, f32[1,2,512,512]{3,2,1,0:T(8,128)S(1)}, s32[]{:T(128)}, f32[16,1,2,512,512]{4,3,2,1,0:T(8,128)}, s32[]{:T(128)}, /*index=5*/s32[]{:T(128)}, s32[]{:T(128)}, s32[]{:T(128)}) while((s32[]{:T(128)}, f32[1,2,512,512]{3,2,1,0:T(8,128)S(1)}, s32[]{:T(128)}, f32[16,1,2,512,512]{4,3,2,1,0:T(8,128)}, s32[]{:T(128)}, ...), condition=%wide.region_1.2_spmd, body=%wide.region_0.1_spmd.sunk | while | flops 6443499520 | bytes 23068808 | solution.py:18
  282.8 1.9 fusion.101
  284.7 1.9 fusion.102
  288.4 1.9 fusion.100
  294.1 1.9 fusion.102
  297.8 1.9 fusion.100
  303.5 1.9 fusion.102
  305.4 1.9 fusion.99
  307.3 1.9 fusion.100
  311.1 1.9 fusion.101
  313.0 1.9 fusion.102
  316.7 1.9 fusion.100
  320.5 1.9 fusion.101
  322.4 1.9 fusion.102
  324.3 1.9 fusion.99
  326.1 1.9 fusion.100
  330.0 1.9 fusion.101
  331.8 1.9 fusion.102
  333.7 1.9 fusion.99
  335.5 1.9 fusion.100
  339.4 1.9 fusion.101
  341.2 1.9 fusion.102
  343.1 1.9 fusion.99
  345.0 1.9 fusion.100
  350.7 1.9 fusion.102
  352.5 1.9 fusion.99
  354.4 1.9 fusion.100
  358.2 1.9 fusion.101
  360.1 1.9 fusion.102
  362.0 1.9 fusion.99
  363.8 1.9 fusion.100
  367.7 1.9 fusion.101
  369.5 1.9 fusion.102
  373.3 1.9 fusion.100
  379.0 1.9 fusion.102
  382.7 1.9 fusion.100
  388.4 1.9 fusion.102
  392.1 1.9 fusion.100
  397.8 1.9 fusion.102
  399.7 1.9 fusion.99
  401.6 1.9 fusion.100
  405.4 1.9 fusion.101
  407.3 1.9 fusion.102
  411.0 1.9 fusion.100
  414.8 1.9 fusion.101
  416.7 1.9 fusion.102
  420.4 1.9 fusion.100
  441.1 24.2 %reduce-scatter.4.cloned.1.call-done = f32[64,4]{1,0:T(8,128)} async-done(((f32[512,4]{1,0:T(8,128)}), f32[64,4]{1,0:T(8,128)}) %reduce-scatter.4.cloned.1.call-update) | async-done | bytes 1040
  (98 shorter events, 78.6 us)
Async XLA Ops:
  6.5 274.5 %all-gather.3.cloned.1.call-start = ((), (), s32[]{:S(2)}) async-start(), calls=%async_computation.1 | async-start | bytes 35651584 | tf_op jit(solution)/shard_map/all_gather | solution.py:11
  49.0 14.9 %copy-start = (f32[1,2,512,512]{2,3,1,0:T(8,128)}, f32[1,2,512,512]{2,3,1,0:T(8,128)S(1)}, u32[]{:S(2)}) copy-start(f32[1,2,512,512]{2,3,1,0:T(8,128)S(1)} %get-tuple-element.80) | copy-start | bytes 6291460
  49.0 14.9 %copy-start.6 = (f32[1,2,512,512]{2,3,1,0:T(8,128)}, f32[1,2,512,512]{2,3,1,0:T(8,128)S(1)}, u32[]{:S(2)}) copy-start(f32[1,2,512,512]{2,3,1,0:T(8,128)S(1)} %get-tuple-element.81) | copy-start | bytes 6291460
  49.0 24.2 %copy-start.2 = (f32[1,2,512,512]{2,3,1,0:T(8,128)}, f32[1,2,512,512]{2,3,1,0:T(8,128)S(1)}, u32[]{:S(2)}) copy-start(f32[1,2,512,512]{2,3,1,0:T(8,128)S(1)} %get-tuple-element.79) | copy-start | bytes 6291460
  49.0 28.0 %copy-start.4 = (f32[1,2,512,512]{2,3,1,0:T(8,128)}, f32[1,2,512,512]{2,3,1,0:T(8,128)S(1)}, u32[]{:S(2)}) copy-start(f32[1,2,512,512]{2,3,1,0:T(8,128)S(1)} %get-tuple-element.78) | copy-start | bytes 6291460
  80.4 384.9 %reduce-scatter.4.cloned.1.call-start = ((), (), s32[]{:S(2)}) async-start(), calls=%async_computation.2 | async-start | bytes 294912
  281.0 141.7 %copy-start.8 = (f32[1,2,512,64]{2,3,1,0:T(8,128)S(1)}, f32[1,2,512,64]{2,3,1,0:T(8,128)}, u32[]{:S(2)}) copy-start(f32[1,2,512,64]{2,3,1,0:T(8,128)} %param.10) | copy-start | bytes 786436
  422.7 3.5 copy-start.5
  426.9 2.7 copy-start.3
  430.5 2.4 copy-start.1
  433.7 2.4 copy-start.7
Sparse Core Ops, SparseCore 0:
  80.5 200.4 all-gather.2
  441.2 24.0 reduce-scatter.3
where the time goes:
time: 482 us; the launch traced here: 474 us
  waiting for transfers between devices  224 us (46%)
  matrix products  188 us (39%)
  local copies, waits for them, and re-layouts  41.3 us (9%)
  between operations  14.6 us (3%)
  other arithmetic  5.32 us (1%)
    all_gather x1, waiting for transfers between devices, carried_in(): gathered = lax.all_gather(part, axis)  200 us
    dot_general x92, matrix products, product(): jnp.einsum('eij,ejk->eik', first_op, second_op, precision=highest, prefer...  158 us
    dot_general x1, matrix products, shards(): jnp.einsum('ebcij,bjk->ebcik', green_left, used_coupling, precision=lax.P...  29.5 us
    squeeze x15, local copies, waits for them, and re-layouts, one(): return combine(state, lax.dynamic_index_in_dim(gathered, source, 0, False))  26.5 us
    unnamed x3, waiting for transfers between devices  24.2 us
    mul x2, local copies, waits for them, and re-layouts, shards(): coupling.reshape(blocks, tile_count, tile_size, tile_count, tile_size)  11.3 us
  transfers between devices with their start and end apart: 2, of which 2 were waited for; matrix products, arithmetic and copies ran while one was open for 0% of the time, Pallas kernels for 0%

commit v1 on v0

v1 whole, which is shorter than its diff:
```python
import functools

import jax
import jax.numpy as jnp
from jax import lax
from jax.experimental import pallas as pl
from jax.experimental.pallas import tpu as pltpu
from jax.sharding import PartitionSpec as P

MESH = pl.DeviceIdType.MESH
NN = (((1,), (0,)), ((), ()))
NT = (((1,), (1,)), ((), ()))
ROWS = 8


def split(value):
    high = value.astype(jnp.bfloat16)
    return high, (value - high.astype(jnp.float32)).astype(jnp.bfloat16)


def dot(left, right, dims=NN):
    return lax.dot_general(left, right, dims, preferred_element_type=jnp.float32)


def product(left_high, left_low, right_high, right_low, dims=NN):
    return dot(left_high, right_high, dims) + dot(left_high, right_low, dims) + dot(left_low, right_high, dims)


def narrow_product(wave, right_high, right_low, dims=NN):
    rows = wave.shape[0]
    high, low = split(wave)
    both = dot(jnp.concatenate([high, low], axis=0), right_high, dims)
    return both[:rows] + both[rows:] + dot(high, right_low, dims)


def combine(mixed, count, orbitals):
    mixed = mixed.reshape(count, 2, ROWS, 2 * orbitals)
    real_part = mixed[:, 0, :, :orbitals] - mixed[:, 1, :, orbitals:]
    imag_part = mixed[:, 0, :, orbitals:] + mixed[:, 1, :, :orbitals]
    return jnp.stack([real_part, imag_part], axis=1).reshape(count * 2 * ROWS, orbitals)


def kernel(
    sizes,
    green_hbm,
    coupling_hbm,
    pattern_hbm,
    injection_hbm,
    weights_hbm,
    out_ref,
    green,
    coupling,
    pattern,
    injection,
    weights,
    high,
    low,
    wave_in,
    wave_out,
    part_out,
    part_in,
    load_sem,
    small_sem,
    send_sem,
    recv_sem,
    part_send_sem,
    part_recv_sem,
):
    energies, places, blocks, orbitals, tiles, modes = sizes
    chunks = modes // ROWS
    tile = orbitals // tiles
    energy = lax.axis_index("energy")
    place = lax.axis_index("length")
    last = places - 1

    def load(block):
        return (
            pltpu.make_async_copy(coupling_hbm.at[block], coupling.at[block], load_sem.at[0, block]),
            pltpu.make_async_copy(green_hbm.at[0, block], green.at[block], load_sem.at[1, block]),
        )

    smalls = (
        pltpu.make_async_copy(pattern_hbm, pattern, small_sem.at[0]),
        pltpu.make_async_copy(injection_hbm.at[0], injection, small_sem.at[1]),
        pltpu.make_async_copy(weights_hbm, weights, small_sem.at[2]),
    )
    smalls[0].start()
    smalls[1].start()
    for block in reversed(range(blocks)):
        for copy in load(block):
            copy.start()
    smalls[2].start()

    barrier = pltpu.get_barrier_semaphore()
    ahead = lax.rem(place + last, places)
    behind = lax.rem(place + 1, places)
    for other in (ahead, behind):
        pl.semaphore_signal(barrier, inc=1, device_id=(energy, other), device_id_type=MESH)
    for hop in range(1, energies):
        other = lax.rem(energy + hop, energies)
        pl.semaphore_signal(barrier, inc=1, device_id=(other, place), device_id_type=MESH)

    def pass_on(chunk):
        return pltpu.make_async_remote_copy(
            src_ref=wave_out.at[chunk],
            dst_ref=wave_in.at[chunk],
            send_sem=send_sem.at[chunk],
            recv_sem=recv_sem.at[chunk],
            device_id=(energy, ahead),
            device_id_type=MESH,
        )

    smalls[0].wait()
    smalls[1].wait()
    smalls[2].wait()

    tile_row = lax.broadcasted_iota(jnp.int32, (tiles, orbitals), 0)
    column = lax.broadcasted_iota(jnp.int32, (tiles, orbitals), 1)
    offset = column - tile_row * tile
    spread = jnp.where(jnp.logical_and(offset >= 0, offset < tile), 1.0, 0.0).astype(jnp.bfloat16)

    def used_coupling(block):
        mask = dot(pattern[block].astype(jnp.float32).astype(jnp.bfloat16), spread)
        used = coupling[block].reshape(tiles, tile, orbitals) * mask[:, None, :]
        return used.reshape(orbitals, orbitals)

    def green_parts(block):
        return split(green[block].reshape(2 * orbitals, orbitals))

    @pl.when(place == last)
    def _():
        for part in range(2):
            rows = injection[part].T.reshape(chunks, ROWS, orbitals)
            wave_in[:, part * ROWS : (part + 1) * ROWS, :] = rows
        wave_out[...] = wave_in[...]

        def direct(index, carry):
            block = blocks - 1 - index
            for copy in load(block):
                copy.wait()
            wave = wave_out[...].reshape(chunks * 2 * ROWS, orbitals)
            mixed = narrow_product(wave, *split(used_coupling(block)), NT)
            moved = combine(narrow_product(mixed, *green_parts(block), NT), chunks, orbitals)
            wave_out[...] = moved.reshape(chunks, 2 * ROWS, orbitals)
            return carry

        lax.fori_loop(0, blocks, direct, 0)
        pl.semaphore_wait(barrier, energies + 1)
        for chunk in range(chunks):
            pass_on(chunk).start()

    def propagator(index, carry):
        block = blocks - 1 - index

        @pl.when(place < last)
        def _():
            for copy in load(block):
                copy.wait()

        turned = split(used_coupling(block).T)
        value = product(*turned, *green_parts(block), NT)
        parts = split(value)
        high[block] = parts[0]
        low[block] = parts[1]
        return carry

    lax.fori_loop(0, blocks, propagator, 0)

    full = last - 3

    @pl.when(place <= full)
    def _():
        def compose(index, carry):
            first = jnp.where(index == 2, 4, 3 - 2 * index)
            second = jnp.where(index == 2, 5, 2 - 2 * index)
            target = 4 + index
            right = (high[second], low[second])
            real_rows = product(high[first, :, :orbitals], low[first, :, :orbitals], *right)
            imag_rows = product(high[first, :, orbitals:], low[first, :, orbitals:], *right)
            real_part = split(real_rows[:, :orbitals] - imag_rows[:, orbitals:])
            high[target, :, :orbitals] = real_part[0]
            low[target, :, :orbitals] = real_part[1]
            imag_part = split(real_rows[:, orbitals:] + imag_rows[:, :orbitals])
            high[target, :, orbitals:] = imag_part[0]
            low[target, :, orbitals:] = imag_part[1]
            return carry

        lax.fori_loop(0, 3, compose, 0)

    @pl.when(place < last)
    def _():
        pl.semaphore_wait(barrier, energies + 1)

    half = chunks // 2

    @pl.when(jnp.logical_and(place < last, place > full))
    def _():
        for start in (0, half):
            for chunk in range(start, start + half):
                pass_on(chunk).wait_recv()
            wave = wave_in[start : start + half].reshape(half * 2 * ROWS, orbitals)
            for block in reversed(range(blocks)):
                wave = combine(narrow_product(wave, high[block], low[block]), half, orbitals)
            wave_out[start : start + half] = wave.reshape(half, 2 * ROWS, orbitals)
            for chunk in range(start, start + half):
                pass_on(chunk).start()

    @pl.when(jnp.logical_and(place > 0, place <= full))
    def _():
        def hop(chunk, carry):
            pass_on(chunk).wait_recv()
            wave_out[chunk] = combine(narrow_product(wave_in[chunk], high[6], low[6]), 1, orbitals)
            pass_on(chunk).start()
            return carry

        lax.fori_loop(0, chunks, hop, 0)

    @pl.when(place == 0)
    def _():
        for chunk in range(chunks):
            pass_on(chunk).wait_recv()

    def own(index, wave):
        block = blocks - 1 - index
        wave = combine(narrow_product(wave, high[block], low[block]), chunks, orbitals)
        charge = jnp.sum(wave * wave, axis=0, keepdims=True) * (weights[0] / (modes * energies))
        width = orbitals // energies
        for target in range(energies):
            piece = charge[:, target * width : (target + 1) * width]
            part_out[target, pl.ds(block, 1), :width] = piece
        return wave

    lax.fori_loop(0, blocks, own, wave_in[...].reshape(chunks * 2 * ROWS, orbitals))

    def give(hop):
        other = lax.rem(energy + hop, energies)
        return pltpu.make_async_remote_copy(
            src_ref=part_out.at[other],
            dst_ref=part_in.at[hop],
            send_sem=part_send_sem.at[hop],
            recv_sem=part_recv_sem.at[hop],
            device_id=(other, place),
            device_id_type=MESH,
        )

    for hop in range(1, energies):
        give(hop).start()
    total = part_out[energy]
    for hop in range(1, energies):
        give(hop).wait_recv()
        total = total + part_in[hop]
    out_ref[...] = total[:blocks, : orbitals // energies]
    for hop in range(1, energies):
        give(hop).wait_send()

    @pl.when(place > 0)
    def _():
        for chunk in range(chunks):
            pass_on(chunk).wait_send()


def shards(places, energies, green_left, coupling, pattern, injection, weights):
    blocks, orbitals, _ = coupling.shape
    tiles = pattern.shape[1]
    modes = injection.shape[3]
    chunks = modes // ROWS
    sizes = (energies, places, blocks, orbitals, tiles, modes)
    anywhere = pl.BlockSpec(memory_space=pl.ANY)
    return pl.pallas_call(
        functools.partial(kernel, sizes),
        out_shape=jax.ShapeDtypeStruct((blocks, orbitals // energies), jnp.float32),
        in_specs=[anywhere] * 5,
        out_specs=pl.BlockSpec(memory_space=pltpu.VMEM),
        scratch_shapes=[
            pltpu.VMEM((blocks, 2, orbitals, orbitals), jnp.float32),
            pltpu.VMEM((blocks, orbitals, orbitals), jnp.float32),
            pltpu.VMEM(pattern.shape, jnp.int32),
            pltpu.VMEM((2, orbitals, modes), jnp.float32),
            pltpu.SMEM((1,), jnp.float32),
            pltpu.VMEM((7, orbitals, 2 * orbitals), jnp.bfloat16),
            pltpu.VMEM((7, orbitals, 2 * orbitals), jnp.bfloat16),
            pltpu.VMEM((chunks, 2 * ROWS, orbitals), jnp.float32),
            pltpu.VMEM((chunks, 2 * ROWS, orbitals), jnp.float32),
            pltpu.VMEM((energies, 8, 128), jnp.float32),
            pltpu.VMEM((energies, 8, 128), jnp.float32),
            pltpu.SemaphoreType.DMA((2, blocks)),
            pltpu.SemaphoreType.DMA((3,)),
            pltpu.SemaphoreType.DMA((chunks,)),
            pltpu.SemaphoreType.DMA((chunks,)),
            pltpu.SemaphoreType.DMA((energies,)),
            pltpu.SemaphoreType.DMA((energies,)),
        ],
        compiler_params=pltpu.CompilerParams(
            collective_id=0, has_side_effects=True, vmem_limit_bytes=56 * 1024 * 1024
        ),
    )(green_left, coupling, pattern, injection, weights)


def solution(mesh):
    placed = (
        P("energy", "length", None, None, None),
        P("length", None, None),
        P("length", None, None),
        P("energy", None, None, None),
        P("energy"),
    )
    return jax.shard_map(
        functools.partial(shards, mesh.shape["length"], mesh.shape["energy"]),
        mesh=mesh,
        in_specs=placed,
        out_specs=P("length", "energy"),
        check_vma=False,
    )
```

time: 482 us -> 90 us (0.19); the launches traced: 474 us -> 89.8 us
  waiting for transfers between devices: 224 us -> 0 us
  matrix products: 188 us -> 0 us
  Pallas kernels: 0 us -> 86 us
  local copies, waits for them, and re-layouts: 41.3 us -> 3.21 us
  between operations: 14.6 us -> 0.66 us
  other arithmetic: 5.32 us -> 0 us
    all_gather x1 -> x0, waiting for transfers between devices: 200 us -> none  [carried_in(): gathered = lax.all_gather(part, axis)]
    dot_general x93 -> x0, matrix products: 188 us -> none  [the longest x92 158 us: product(): jnp.einsum('eij,ejk->eik', first_op, second_op, precision=highest, prefer...]
    pallas_call x0 -> x1, Pallas kernels: none -> 86 us  [shards(): pl.pallas_call(functools.partial(kernel, sizes), out_shape=jax.ShapeDtype...]
    squeeze x16 -> x0, local copies, waits for them, and re-layouts: 27.5 us -> none  [the longest x15 26.5 us: one(): return combine(state, lax.dynamic_index_in_dim(gathered, source, 0, False))]
    unnamed x3 -> x0, waiting for transfers between devices: 24.2 us -> none
    mul x2 -> x0, local copies, waits for them, and re-layouts: 11.3 us -> none  [shards(): coupling.reshape(blocks, tile_count, tile_size, tile_count, tile_size)]
  transfers between devices with their start and end apart: 2 -> 0, of which waited for: 2 -> 0; matrix products, arithmetic and copies ran while one was open for 0% -> 0% of each run, Pallas kernels for 0% -> 0%
where the time goes in v1:
time: 90 us; the launch traced here: 89.8 us
  Pallas kernels  86 us (96%)
  local copies, waits for them, and re-layouts  3.21 us (4%)
    pallas_call x1, Pallas kernels, shards(): pl.pallas_call(functools.partial(kernel, sizes), out_shape=jax.ShapeDtype...  86 us
    unnamed x2, local copies, waits for them, and re-layouts  3.21 us

profile of v1, /device:TPU:1, one launch (start us, length us, event | category | flops | bytes accessed | tf_op | source)
XLA Modules:
  0.0 89.8 jit_solution(15402200523381708825)
XLA Ops:
  0.7 1.9 %copy.6.injection_hbm = f32[1,2,512,64]{3,2,1,0:T(8,128)} copy(f32[1,2,512,64]{2,3,1,0:T(8,128)} %param.8) | data formatting | bytes 524288 | tf_op args[3]
  2.6 86.0 %shard_map.55 = f32[4,64]{1,0:T(4,128)} custom-call(f32[1,4,2,512,512]{4,3,2,1,0:T(8,128)} %green_hbm.1, f32[4,512,512]{2,1,0:T(8,128)} %coupling_hbm.1, s32[4,8,8]{2,1,0:T(8,128)} %pattern_hbm.1, f32[1,2,512,64]{3,2,1,0:T(8,128)} %copy.6.injection_hbm, f32[1]{0:T(128)S(6)} %copy.8.weights_hbm), custom_call_target="tpu_custom_call" | custom-call | tf_op jit(solution)/shard_map/pallas_call | solution.py:269
  88.6 1.3 %copy.9 = f32[4,64]{1,0:T(4,128)} copy(f32[4,64]{1,0:T(4,128)} %shard_map.55) | data formatting | bytes 2048

commit v2 on v1

v2 whole, which is shorter than its diff:
```python
import functools

import jax
import jax.numpy as jnp
from jax import lax
from jax.experimental import pallas as pl
from jax.experimental.pallas import tpu as pltpu
from jax.sharding import PartitionSpec as P

MESH = pl.DeviceIdType.MESH
NN = (((1,), (0,)), ((), ()))
NT = (((1,), (1,)), ((), ()))
ROWS = 4


def split(value):
    high = value.astype(jnp.bfloat16)
    return high, (value - high.astype(jnp.float32)).astype(jnp.bfloat16)


def dot(left, right, dims=NN):
    return lax.dot_general(left, right, dims, preferred_element_type=jnp.float32)


def product(left_high, left_low, right_high, right_low, dims=NN):
    return dot(left_high, right_high, dims) + dot(left_high, right_low, dims) + dot(left_low, right_high, dims)


def narrow_product(wave, right_high, right_low, dims=NN):
    rows = wave.shape[0]
    high = wave.astype(jnp.bfloat16)
    kept = high.astype(jnp.float32)
    stacked = jnp.concatenate([kept, wave - kept], axis=0).astype(jnp.bfloat16)
    both = dot(stacked, right_high, dims)
    return both[:rows] + both[rows:] + dot(high, right_low, dims)


def combine(mixed, orbitals):
    mixed = mixed.reshape(-1, 2 * ROWS, 2 * orbitals)
    row = lax.broadcasted_iota(jnp.int32, (1, 2 * ROWS, orbitals), 1)
    turned = pltpu.roll(mixed[:, :, orbitals:], ROWS, 1)
    moved = mixed[:, :, :orbitals] + jnp.where(row < ROWS, -turned, turned)
    return moved.reshape(-1, orbitals)


def kernel(
    sizes,
    green_hbm,
    coupling_hbm,
    pattern_hbm,
    injection_hbm,
    weights_hbm,
    out_ref,
    green,
    coupling,
    pattern,
    injection,
    weights,
    high,
    low,
    waves,
    wave_out,
    swapped_in,
    part_out,
    part_in,
    charge,
    load_sem,
    small_sem,
    send_sem,
    recv_sem,
    part_send_sem,
    part_recv_sem,
    forward_send_sem,
    forward_recv_sem,
    swap_send_sem,
    swap_recv_sem,
):
    energies, places, blocks, orbitals, tiles, modes = sizes
    chunks = modes // ROWS
    tile = orbitals // tiles
    energy = lax.axis_index("energy")
    place = lax.axis_index("length")
    last = places - 1
    full = last - 2
    wave_in = waves.at[0]
    sibling = energy + 1 - 2 * lax.rem(energy, 2)

    def swaps(where):
        inside = jnp.logical_and(where > 0, where < full)
        return jnp.logical_and(inside, lax.rem(full + 1 - where, 2) == 0)

    swapped = swaps(place)
    sends_to = jnp.where(swapped != swaps(place - 1), sibling, energy)
    sent_by = jnp.where(swapped != swaps(place + 1), sibling, energy)

    def load(block):
        return (
            pltpu.make_async_copy(coupling_hbm.at[block], coupling.at[block], load_sem.at[0, block]),
            pltpu.make_async_copy(green_hbm.at[0, block], green.at[block], load_sem.at[1, block]),
        )

    smalls = (
        pltpu.make_async_copy(pattern_hbm, pattern, small_sem.at[0]),
        pltpu.make_async_copy(injection_hbm.at[0], injection, small_sem.at[1]),
        pltpu.make_async_copy(weights_hbm, weights, small_sem.at[2]),
    )
    smalls[0].start()
    smalls[1].start()
    for copy in load(blocks - 1):
        copy.start()
    smalls[2].start()

    barrier = pltpu.get_barrier_semaphore()
    ahead = lax.rem(place + last, places)
    behind = lax.rem(place + 1, places)
    pl.semaphore_signal(barrier, inc=1, device_id=(sends_to, ahead), device_id_type=MESH)
    pl.semaphore_signal(barrier, inc=1, device_id=(sent_by, behind), device_id_type=MESH)
    for hop in range(1, energies):
        other = lax.rem(energy + hop, energies)
        pl.semaphore_signal(barrier, inc=1, device_id=(other, place), device_id_type=MESH)

    def pass_on(chunk):
        return pltpu.make_async_remote_copy(
            src_ref=wave_out.at[chunk],
            dst_ref=wave_in.at[chunk],
            send_sem=send_sem.at[chunk],
            recv_sem=recv_sem.at[chunk],
            device_id=(sends_to, ahead),
            device_id_type=MESH,
        )

    def forward(chunk):
        return pltpu.make_async_remote_copy(
            src_ref=waves.at[0, chunk],
            dst_ref=waves.at[1, chunk],
            send_sem=forward_send_sem.at[chunk],
            recv_sem=forward_recv_sem.at[chunk],
            device_id=(sibling, place),
            device_id_type=MESH,
        )

    def swap(part):
        return pltpu.make_async_remote_copy(
            src_ref=green.at[0, part],
            dst_ref=swapped_in.at[part],
            send_sem=swap_send_sem.at[part],
            recv_sem=swap_recv_sem.at[part],
            device_id=(sibling, place),
            device_id_type=MESH,
        )

    def arrive(block):
        for copy in load(block):
            copy.wait()

        @pl.when(block > 1)
        def _():
            for copy in load(block - 2):
                copy.start()

    smalls[0].wait()
    smalls[1].wait()
    for copy in load(blocks - 2):
        copy.start()

    tile_row = lax.broadcasted_iota(jnp.int32, (tiles, orbitals), 0)
    column = lax.broadcasted_iota(jnp.int32, (tiles, orbitals), 1)
    offset = column - tile_row * tile
    spread = jnp.where(jnp.logical_and(offset >= 0, offset < tile), 1.0, 0.0).astype(jnp.bfloat16)

    def used_coupling(block):
        mask = dot(pattern[block].astype(jnp.float32).astype(jnp.bfloat16), spread)
        used = coupling[block].reshape(tiles, tile, orbitals) * mask[:, None, :]
        return used.reshape(orbitals, orbitals)

    def green_parts(block):
        return split(green[block].reshape(2 * orbitals, orbitals))

    @pl.when(place == last)
    def _():
        for chunk in range(chunks):
            for part in range(2):
                rows = injection[part, chunk * ROWS : (chunk + 1) * ROWS, :]
                wave_in[chunk, part * ROWS : (part + 1) * ROWS, :] = rows
        wave = wave_in[...].reshape(chunks * 2 * ROWS, orbitals)
        for block in reversed(range(blocks)):
            arrive(block)
            mixed = narrow_product(wave, *split(used_coupling(block)), NT)
            wave = combine(narrow_product(mixed, *green_parts(block), NT), orbitals)
        wave_out[...] = wave.reshape(chunks, 2 * ROWS, orbitals)
        pl.semaphore_wait(barrier, energies + 1)
        for chunk in range(chunks):
            pass_on(chunk).start()

    def propagator(index, carry):
        block = blocks - 1 - index

        @pl.when(place < last)
        def _():
            arrive(block)

        turned = split(used_coupling(block).T)
        value = product(*turned, *green_parts(block), NT)
        parts = split(value)
        high[block] = parts[0]
        low[block] = parts[1]
        return carry

    lax.fori_loop(0, blocks, propagator, 0)

    @pl.when(place <= full)
    def _():
        def compose(index, carry):
            first = jnp.where(index >= 2, 4, 3 - 2 * index)
            second = jnp.where(index >= 2, jnp.where(index == 2, 5, 1), 2 - 2 * index)
            target = jnp.where(index == 3, 5, 4 + index)
            right = (high[second], low[second])
            real_rows = product(high[first, :, :orbitals], low[first, :, :orbitals], *right)
            imag_rows = product(high[first, :, orbitals:], low[first, :, orbitals:], *right)
            real_part = split(real_rows[:, :orbitals] - imag_rows[:, orbitals:])
            high[target, :, :orbitals] = real_part[0]
            low[target, :, :orbitals] = real_part[1]
            imag_part = split(real_rows[:, orbitals:] + imag_rows[:, :orbitals])
            high[target, :, orbitals:] = imag_part[0]
            low[target, :, orbitals:] = imag_part[1]
            return carry

        lax.fori_loop(0, jnp.where(place <= 1, 4, 3), compose, 0)

    @pl.when(place < last)
    def _():
        pl.semaphore_wait(barrier, energies + 1)

    @pl.when(swapped)
    def _():
        for part in range(2):
            columns = slice(part * orbitals, (part + 1) * orbitals)
            green[0, part] = high[6, :, columns].astype(jnp.float32) + low[6, :, columns].astype(jnp.float32)
            swap(part).start()
        for part in range(2):
            columns = slice(part * orbitals, (part + 1) * orbitals)
            swap(part).wait_recv()
            parts = split(swapped_in[part])
            high[6, :, columns] = parts[0]
            low[6, :, columns] = parts[1]

    half = chunks // 2

    def half_hop(maps):
        for start in (0, half):
            for chunk in range(start, start + half):
                pass_on(chunk).wait_recv()
            wave = wave_in[start : start + half].reshape(half * 2 * ROWS, orbitals)
            for block in maps:
                wave = combine(narrow_product(wave, high[block], low[block]), orbitals)
            wave_out[start : start + half] = wave.reshape(half, 2 * ROWS, orbitals)
            for chunk in range(start, start + half):
                pass_on(chunk).start()

    @pl.when(jnp.logical_and(place < last, place > full))
    def _():
        half_hop(tuple(reversed(range(blocks))))

    @pl.when(place == full)
    def _():
        half_hop((6,))

    @pl.when(jnp.logical_and(place > 0, place < full))
    def _():
        def hop(chunk, carry):
            pass_on(chunk).wait_recv()
            wave_out[chunk] = combine(narrow_product(wave_in[chunk], high[6], low[6]), orbitals)
            pass_on(chunk).start()

            @pl.when(swapped)
            def _():
                forward(chunk).start()

            return carry

        lax.fori_loop(0, chunks, hop, 0, unroll=True)

    smalls[2].wait()
    factor = weights[0] / (modes * energies)

    def density(wave):
        return jnp.sum(wave * wave, axis=0, keepdims=True) * factor

    def own(part, carry):
        @pl.when(swapped)
        def _():
            for chunk in range(half):
                forward(part * half + chunk).wait_recv()

        wave = waves[jnp.where(swapped, 1, 0), pl.ds(part * half, half)].reshape(half * 2 * ROWS, orbitals)
        for block in reversed(range(blocks)):
            wave = combine(narrow_product(wave, high[block], low[block]), orbitals)
            charge[part, block : block + 1, :] = density(wave)
        return carry

    def own_at_end(part, carry):
        @pl.when(place == 0)
        def _():
            for chunk in range(half):
                pass_on(part * half + chunk).wait_recv()

        wave = waves[0, pl.ds(part * half, half)].reshape(half * 2 * ROWS, orbitals)
        for block in range(blocks):
            slot = 6 - block
            moved = combine(narrow_product(wave, high[slot], low[slot]), orbitals)
            charge[part, block : block + 1, :] = density(moved)
        return carry

    @pl.when(place > 1)
    def _():
        lax.fori_loop(0, 2, own, 0)

    @pl.when(place <= 1)
    def _():
        lax.fori_loop(0, 2, own_at_end, 0)

    width = orbitals // energies
    summed = charge[0] + charge[1]
    for target in range(energies):
        part_out[target, :blocks, :width] = summed[:, target * width : (target + 1) * width]

    def give(hop):
        other = lax.rem(energy + hop, energies)
        return pltpu.make_async_remote_copy(
            src_ref=part_out.at[other],
            dst_ref=part_in.at[hop],
            send_sem=part_send_sem.at[hop],
            recv_sem=part_recv_sem.at[hop],
            device_id=(other, place),
            device_id_type=MESH,
        )

    for hop in range(1, energies):
        give(hop).start()
    total = part_out[energy]
    for hop in range(1, energies):
        give(hop).wait_recv()
        total = total + part_in[hop]
    out_ref[...] = total[:blocks, : orbitals // energies]
    for hop in range(1, energies):
        give(hop).wait_send()

    @pl.when(place > 0)
    def _():
        for chunk in range(chunks):
            pass_on(chunk).wait_send()

    @pl.when(swapped)
    def _():
        for chunk in range(chunks):
            forward(chunk).wait_send()
        for part in range(2):
            swap(part).wait_send()


def shards(places, energies, green_left, coupling, pattern, injection, weights):
    blocks, orbitals, _ = coupling.shape
    tiles = pattern.shape[1]
    modes = injection.shape[3]
    chunks = modes // ROWS
    sizes = (energies, places, blocks, orbitals, tiles, modes)
    return pl.pallas_call(
        functools.partial(kernel, sizes),
        out_shape=pltpu.VMEM((blocks, orbitals // energies), jnp.float32),
        in_specs=[pl.BlockSpec(memory_space=pltpu.HBM)] * 5,
        out_specs=pl.BlockSpec(memory_space=pltpu.VMEM),
        scratch_shapes=[
            pltpu.VMEM((blocks, 2, orbitals, orbitals), jnp.float32),
            pltpu.VMEM((blocks, orbitals, orbitals), jnp.float32),
            pltpu.VMEM(pattern.shape, jnp.int32),
            pltpu.VMEM((2, modes, orbitals), jnp.float32),
            pltpu.SMEM((1,), jnp.float32),
            pltpu.VMEM((7, orbitals, 2 * orbitals), jnp.bfloat16),
            pltpu.VMEM((7, orbitals, 2 * orbitals), jnp.bfloat16),
            pltpu.VMEM((2, chunks, 2 * ROWS, orbitals), jnp.float32),
            pltpu.VMEM((chunks, 2 * ROWS, orbitals), jnp.float32),
            pltpu.VMEM((2, orbitals, orbitals), jnp.float32),
            pltpu.VMEM((energies, 8, 128), jnp.float32),
            pltpu.VMEM((energies, 8, 128), jnp.float32),
            pltpu.VMEM((2, blocks, orbitals), jnp.float32),
            pltpu.SemaphoreType.DMA((2, blocks)),
            pltpu.SemaphoreType.DMA((3,)),
            pltpu.SemaphoreType.DMA((chunks,)),
            pltpu.SemaphoreType.DMA((chunks,)),
            pltpu.SemaphoreType.DMA((energies,)),
            pltpu.SemaphoreType.DMA((energies,)),
            pltpu.SemaphoreType.DMA((chunks,)),
            pltpu.SemaphoreType.DMA((chunks,)),
            pltpu.SemaphoreType.DMA((2,)),
            pltpu.SemaphoreType.DMA((2,)),
        ],
        compiler_params=pltpu.CompilerParams(
            collective_id=0, has_side_effects=True, vmem_limit_bytes=56 * 1024 * 1024
        ),
    )(green_left, coupling, pattern, jnp.swapaxes(injection, 2, 3), weights)


def solution(mesh):
    placed = (
        P("energy", "length", None, None, None),
        P("length", None, None),
        P("length", None, None),
        P("energy", None, None, None),
        P("energy"),
    )
    return jax.shard_map(
        functools.partial(shards, mesh.shape["length"], mesh.shape["energy"]),
        mesh=mesh,
        in_specs=placed,
        out_specs=P("length", "energy"),
        check_vma=False,
    )
```

time: 90 us -> 78.3 us (0.87)
  Pallas kernels: 86 us -> 76.9 us
  local copies, waits for them, and re-layouts: 3.21 us -> 0.58 us
    pallas_call x1, Pallas kernels: 86 us -> 76.9 us  [shards(): pl.pallas_call(functools.partial(kernel, sizes), out_shape=pltpu.VMEM((bl...]
    unnamed x2 -> x1, local copies, waits for them, and re-layouts: 3.21 us -> 0.58 us
where the time goes in v2:
time: 78.3 us; the launch traced here: 78.1 us
  Pallas kernels  76.9 us (98%)
    pallas_call x1, Pallas kernels, shards(): pl.pallas_call(functools.partial(kernel, sizes), out_shape=pltpu.VMEM((bl...  76.9 us

profile of v2, /device:TPU:1, one launch (start us, length us, event | category | flops | bytes accessed | tf_op | source)
XLA Modules:
  0.0 78.1 jit_solution(7335355594185467836)
XLA Ops:
  0.7 76.9 %shard_map.55 = f32[4,64]{1,0:T(4,128)S(1)} custom-call(f32[1,4,2,512,512]{4,3,2,1,0:T(8,128)} %green_hbm.1, f32[4,512,512]{2,1,0:T(8,128)} %coupling_hbm.1, s32[4,8,8]{2,1,0:T(8,128)} %pattern_hbm.1, f32[1,2,64,512]{3,2,1,0:T(8,128)} %bitcast.1, f32[1]{0:T(128)S(6)} %copy.8.weights_hbm), custom_call_target="tpu_custom_call" | custom-call | tf_op jit(solution)/shard_map/pallas_call | solution.py:367
  77.5 0.6 copy.7

commit v3 on v2

--- a/solution.py
+++ b/solution.py
@@ -93,11 +93,10 @@
     sends_to = jnp.where(swapped != swaps(place - 1), sibling, energy)
     sent_by = jnp.where(swapped != swaps(place + 1), sibling, energy)
 
-    def load(block):
-        return (
-            pltpu.make_async_copy(coupling_hbm.at[block], coupling.at[block], load_sem.at[0, block]),
-            pltpu.make_async_copy(green_hbm.at[0, block], green.at[block], load_sem.at[1, block]),
-        )
+    def load(block, kind):
+        if kind == 0:
+            return pltpu.make_async_copy(coupling_hbm.at[block], coupling.at[block], load_sem.at[0, block])
+        return pltpu.make_async_copy(green_hbm.at[0, block], green.at[block], load_sem.at[1, block])
 
     smalls = (
         pltpu.make_async_copy(pattern_hbm, pattern, small_sem.at[0]),
@@ -106,8 +105,8 @@
     )
     smalls[0].start()
     smalls[1].start()
-    for copy in load(blocks - 1):
-        copy.start()
+    for kind in range(2):
+        load(blocks - 1, kind).start()
     smalls[2].start()
 
     barrier = pltpu.get_barrier_semaphore()
@@ -149,19 +148,17 @@
             device_id_type=MESH,
         )
 
-    def arrive(block):
-        for copy in load(block):
-            copy.wait()
+    def arrive(block, kind):
+        load(block, kind).wait()
 
         @pl.when(block > 1)
         def _():
-            for copy in load(block - 2):
-                copy.start()
+            load(block - 2, kind).start()
 
     smalls[0].wait()
     smalls[1].wait()
-    for copy in load(blocks - 2):
-        copy.start()
+    for kind in range(2):
+        load(blocks - 2, kind).start()
 
     tile_row = lax.broadcasted_iota(jnp.int32, (tiles, orbitals), 0)
     column = lax.broadcasted_iota(jnp.int32, (tiles, orbitals), 1)
@@ -184,8 +181,9 @@
                 wave_in[chunk, part * ROWS : (part + 1) * ROWS, :] = rows
         wave = wave_in[...].reshape(chunks * 2 * ROWS, orbitals)
         for block in reversed(range(blocks)):
-            arrive(block)
+            arrive(block, 0)
             mixed = narrow_product(wave, *split(used_coupling(block)), NT)
+            arrive(block, 1)
             wave = combine(narrow_product(mixed, *green_parts(block), NT), orbitals)
         wave_out[...] = wave.reshape(chunks, 2 * ROWS, orbitals)
         pl.semaphore_wait(barrier, energies + 1)
@@ -197,7 +195,8 @@
 
         @pl.when(place < last)
         def _():
-            arrive(block)
+            arrive(block, 0)
+            arrive(block, 1)
 
         turned = split(used_coupling(block).T)
         value = product(*turned, *green_parts(block), NT)
@@ -214,13 +213,24 @@
             first = jnp.where(index >= 2, 4, 3 - 2 * index)
             second = jnp.where(index >= 2, jnp.where(index == 2, 5, 1), 2 - 2 * index)
             target = jnp.where(index == 3, 5, 4 + index)
-            right = (high[second], low[second])
-            real_rows = product(high[first, :, :orbitals], low[first, :, :orbitals], *right)
-            imag_rows = product(high[first, :, orbitals:], low[first, :, orbitals:], *right)
-            real_part = split(real_rows[:, :orbitals] - imag_rows[:, orbitals:])
+            def sides(slot):
+                return [
+                    (high[slot, :, side * orbitals : (side + 1) * orbitals], low[slot, :, side * orbitals : (side + 1) * orbitals])
+                    for side in range(2)
+                ]
+
+            def summed_sides(parts):
+                whole = [part[0].astype(jnp.float32) + part[1].astype(jnp.float32) for part in parts]
+                return split(whole[0] + whole[1])
+
+            left, right = sides(first), sides(second)
+            reals = product(*left[0], *right[0])
+            imags = product(*left[1], *right[1])
+            crossed = product(*summed_sides(left), *summed_sides(right))
+            real_part = split(reals - imags)
             high[target, :, :orbitals] = real_part[0]
             low[target, :, :orbitals] = real_part[1]
-            imag_part = split(real_rows[:, orbitals:] + imag_rows[:, :orbitals])
+            imag_part = split(crossed - reals - imags)
             high[target, :, orbitals:] = imag_part[0]
             low[target, :, orbitals:] = imag_part[1]
             return carry
@@ -261,24 +271,21 @@
     def _():
         half_hop(tuple(reversed(range(blocks))))
 
-    @pl.when(place == full)
-    def _():
-        half_hop((6,))
-
-    @pl.when(jnp.logical_and(place > 0, place < full))
-    def _():
-        def hop(chunk, carry):
+    def hops(forwards):
+        for chunk in range(chunks):
             pass_on(chunk).wait_recv()
             wave_out[chunk] = combine(narrow_product(wave_in[chunk], high[6], low[6]), orbitals)
             pass_on(chunk).start()
-
-            @pl.when(swapped)
-            def _():
+            if forwards:
                 forward(chunk).start()
 
-            return carry
-
-        lax.fori_loop(0, chunks, hop, 0, unroll=True)
+    @pl.when(swapped)
+    def _():
+        hops(True)
+
+    @pl.when(jnp.logical_and(jnp.logical_and(place > 0, place <= full), jnp.logical_not(swapped)))
+    def _():
+        hops(False)
 
     smalls[2].wait()
     factor = weights[0] / (modes * energies)

time: 78.3 us -> 77.3 us (0.987)
  Pallas kernels: 76.9 us -> 75.9 us
    pallas_call x1, Pallas kernels: 76.9 us -> 75.9 us  [shards(): pl.pallas_call(functools.partial(kernel, sizes), out_shape=pltpu.VMEM((bl...]
where the time goes in v3:
time: 77.3 us; the launch traced here: 77.1 us
  Pallas kernels  75.9 us (98%)
    pallas_call x1, Pallas kernels, shards(): pl.pallas_call(functools.partial(kernel, sizes), out_shape=pltpu.VMEM((bl...  75.9 us

profile of v3, /device:TPU:1, one launch (start us, length us, event | category | flops | bytes accessed | tf_op | source)
XLA Modules:
  0.0 77.1 jit_solution(8103209923205460148)
XLA Ops:
  0.7 75.9 %shard_map.55 = f32[4,64]{1,0:T(4,128)S(1)} custom-call(f32[1,4,2,512,512]{4,3,2,1,0:T(8,128)} %green_hbm.1, f32[4,512,512]{2,1,0:T(8,128)} %coupling_hbm.1, s32[4,8,8]{2,1,0:T(8,128)} %pattern_hbm.1, f32[1,2,64,512]{3,2,1,0:T(8,128)} %bitcast.1, f32[1]{0:T(128)S(6)} %copy.8.weights_hbm), custom_call_target="tpu_custom_call" | custom-call | tf_op jit(solution)/shard_map/pallas_call | solution.py:374
  76.5 0.6 copy.7

commit v4 on v3

--- a/solution.py
+++ b/solution.py
@@ -180,15 +180,23 @@
                 rows = injection[part, chunk * ROWS : (chunk + 1) * ROWS, :]
                 wave_in[chunk, part * ROWS : (part + 1) * ROWS, :] = rows
         wave = wave_in[...].reshape(chunks * 2 * ROWS, orbitals)
-        for block in reversed(range(blocks)):
+        for block in reversed(range(1, blocks)):
             arrive(block, 0)
             mixed = narrow_product(wave, *split(used_coupling(block)), NT)
             arrive(block, 1)
             wave = combine(narrow_product(mixed, *green_parts(block), NT), orbitals)
-        wave_out[...] = wave.reshape(chunks, 2 * ROWS, orbitals)
+        arrive(0, 0)
+        arrive(0, 1)
         pl.semaphore_wait(barrier, energies + 1)
-        for chunk in range(chunks):
-            pass_on(chunk).start()
+        used, greens = split(used_coupling(0)), green_parts(0)
+        rows = modes
+        for side in range(2):
+            mixed = narrow_product(wave[side * rows : (side + 1) * rows], *used, NT)
+            moved = combine(narrow_product(mixed, *greens, NT), orbitals)
+            first = side * (chunks // 2)
+            wave_out[first : first + chunks // 2] = moved.reshape(chunks // 2, 2 * ROWS, orbitals)
+            for chunk in range(first, first + chunks // 2):
+                pass_on(chunk).start()
 
     def propagator(index, carry):
         block = blocks - 1 - index
@@ -276,8 +284,9 @@
             pass_on(chunk).wait_recv()
             wave_out[chunk] = combine(narrow_product(wave_in[chunk], high[6], low[6]), orbitals)
             pass_on(chunk).start()
-            if forwards:
-                forward(chunk).start()
+            if forwards and chunk % 4 == 3:
+                for earlier in range(chunk - 3, chunk + 1):
+                    forward(earlier).start()
 
     @pl.when(swapped)
     def _():

time: 77.3 us -> 77.3 us (level)
  no operation moved by 1% of the time
where the time goes in v4:
time: 77.3 us; the launch traced here: 77.1 us
  Pallas kernels  75.9 us (98%)
    pallas_call x1, Pallas kernels, shards(): pl.pallas_call(functools.partial(kernel, sizes), out_shape=pltpu.VMEM((bl...  75.9 us

profile of v4, /device:TPU:1, one launch (start us, length us, event | category | flops | bytes accessed | tf_op | source)
XLA Modules:
  0.0 77.1 jit_solution(1748369977715872720)
XLA Ops:
  0.7 75.9 %shard_map.55 = f32[4,64]{1,0:T(4,128)S(1)} custom-call(f32[1,4,2,512,512]{4,3,2,1,0:T(8,128)} %green_hbm.1, f32[4,512,512]{2,1,0:T(8,128)} %coupling_hbm.1, s32[4,8,8]{2,1,0:T(8,128)} %pattern_hbm.1, f32[1,2,64,512]{3,2,1,0:T(8,128)} %bitcast.1, f32[1]{0:T(128)S(6)} %copy.8.weights_hbm), custom_call_target="tpu_custom_call" | custom-call | tf_op jit(solution)/shard_map/pallas_call | solution.py:383
  76.5 0.6 copy.7

commit v5 on v3

--- a/solution.py
+++ b/solution.py
@@ -342,10 +342,11 @@
             device_id_type=MESH,
         )
 
-    for hop in range(1, energies):
+    order = sorted(range(1, energies), key=lambda hop: -min(hop, energies - hop))
+    for hop in order:
         give(hop).start()
     total = part_out[energy]
-    for hop in range(1, energies):
+    for hop in reversed(order):
         give(hop).wait_recv()
         total = total + part_in[hop]
     out_ref[...] = total[:blocks, : orbitals // energies]

time: 77.3 us -> 77.2 us (level)
  no operation moved by 1% of the time
where the time goes in v5:
time: 77.2 us; the launch traced here: 77 us
  Pallas kernels  75.8 us (98%)
    pallas_call x1, Pallas kernels, shards(): pl.pallas_call(functools.partial(kernel, sizes), out_shape=pltpu.VMEM((bl...  75.8 us

profile of v5, /device:TPU:1, one launch (start us, length us, event | category | flops | bytes accessed | tf_op | source)
XLA Modules:
  0.0 77.0 jit_solution(7029815896465226355)
XLA Ops:
  0.7 75.8 %shard_map.55 = f32[4,64]{1,0:T(4,128)S(1)} custom-call(f32[1,4,2,512,512]{4,3,2,1,0:T(8,128)} %green_hbm.1, f32[4,512,512]{2,1,0:T(8,128)} %coupling_hbm.1, s32[4,8,8]{2,1,0:T(8,128)} %pattern_hbm.1, f32[1,2,64,512]{3,2,1,0:T(8,128)} %bitcast.1, f32[1]{0:T(128)S(6)} %copy.8.weights_hbm), custom_call_target="tpu_custom_call" | custom-call | tf_op jit(solution)/shard_map/pallas_call | solution.py:375
  76.4 0.6 copy.7
